TPU v7x, 256 devices: a whole 4x4x8 slice. The times are simulated.
256 devices in a mesh: row: 4 (over y_lo, core), col: 16 (over y_hi, z), layer: 4 (over x).
Axes of the slice: x: 4, y: 4 (y_hi: 2, y_lo: 2; y = y_hi * 2 + y_lo), z: 8, core: 2. Of those that a mesh axis runs over, the one named last changes fastest.
Arguments:
- left_panels: bfloat16 [4, 16, 4, 16, 128, 128], P('row', 'col', 'layer'), may hold values from -6 to 6
- right_panels: bfloat16 [4, 16, 4, 64, 128, 128], P('row', 'col', 'layer'), may hold values from -0.5 to 0.5
- pair_lists: int32 [4, 16, 4, 3, 3, 256], P('row', 'col', 'layer'), may hold values from 0 to 63, as said below
Outputs:
- product_tiles: float32 [4, 16, 16, 128, 128], P('row', 'col', 'layer')
Inputs may be any that keep to these rules, and one draw needn't show every extreme that they name: `pair_lists`: entry 0 of the second to last dimension is an A block below 16, entry 1 a B block below 64, entry 2 a C block below 16 or 16 for an empty slot. At each grid position, layer and step the used slots come first; at least one grid position, layer and step uses all 256 slots.
All inputs are finite; a program needn't handle non-finite values.
Results may differ from a plain program's by a relative error of at most 0.0003.
Values may be sent and summed in bfloat16 or wider, within the bound.
A program may use at most 64 MiB of HBM per device.

v0:
```python
import functools

import jax
import jax.numpy as jnp
from jax import lax
from jax.experimental import pallas as pl
from jax.experimental.pallas import tpu as pltpu
from jax.sharding import PartitionSpec as P

PARTS = 2
UNROLL = 34


def sort_lists(pairs, chunk_lanes, zero_block, block_count):
    slots = pairs.shape[1]
    a_row, b_row, c_row = pairs[0:1], pairs[1:2], pairs[2:3]
    iota = lambda shape, dim: lax.broadcasted_iota(jnp.int32, shape, dim)
    square = (slots, slots)
    c_across = jnp.broadcast_to(c_row, square)
    c_down = jnp.transpose(c_across)
    earlier = iota(square, 0) < iota(square, 1)
    rank = jnp.sum(jnp.where((c_down == c_across) & earlier, 1, 0), axis=0, keepdims=True)
    group = iota((block_count, slots), 0)
    c_short = jnp.broadcast_to(c_row, (block_count, slots))
    counts = jnp.sum(jnp.where(c_short == group, 1, 0), axis=1, keepdims=True)
    halves = jnp.broadcast_to((counts + 1) >> 1, (block_count, slots))
    before = jnp.sum(jnp.where(group < c_short, halves, 0), axis=0, keepdims=True)
    place = jnp.where(c_row < block_count, 2 * before + rank, 1023)
    first = jnp.where(rank == 0, 1, 0)
    word = place + (a_row << 10) + (b_row << 15) + (c_row << 22) + (first << 28)
    down = jnp.transpose(jnp.broadcast_to(word, square))
    if chunk_lanes != slots:
        down = down[:, :chunk_lanes]
    place = down & 1023
    entry = (((down >> 10) & 31) + 1) + (((down >> 15) & 127) << 8) + (((down >> 28) & 1) << 16)
    c_down = (down >> 22) & 63
    lane = iota((slots, chunk_lanes), 1)
    one = jnp.sum(jnp.where(place == 2 * lane, entry, 0), axis=0, keepdims=True)
    two = jnp.sum(jnp.where(place == 2 * lane + 1, entry, 0), axis=0, keepdims=True)
    last = jnp.max(jnp.where((c_down == lane) & (place < 1023), (place >> 1) + 1, 0), axis=0, keepdims=True)
    rows = []
    for picked in (one, two):
        a = picked & 255
        rows.append(jnp.where(a == 0, zero_block, a - 1))
    for picked in (one, two):
        rows.append((picked >> 8) & 255)
    rows.append(1 - ((one >> 16) & 1))
    rows.append(last)
    return rows


def kernel(
    pairs_ref,
    a_hbm,
    b_hbm,
    out_ref,
    *scratch,
    sizes,
):
    n_row, n_col, n_layer, ta, bs, nc, chunks, lanes, unroll = sizes
    rows = bs // PARTS
    scratch = list(scratch)

    def take(count):
        taken = scratch[:count]
        del scratch[:count]
        return taken

    a_bufs = [take(PARTS) for _ in range(3)]
    (b_buf, products) = take(2)
    plan_out = take(3)
    plan_in = take(2)
    plan_s = take(3)
    partial = [take(PARTS) for _ in range(3)]
    far_l = [take(PARTS) for _ in range(3)]
    far_r = [take(PARTS) for _ in range(3)]
    near_l = [take(PARTS) for _ in range(3)]
    near_r = [take(PARTS) for _ in range(3)]
    total = [take(PARTS) for _ in range(3)]
    shift = [take(PARTS) for _ in range(2)]
    local_sem, send_sem, recv_sem = take(3)

    r, q, l = lax.axis_index("row"), lax.axis_index("col"), lax.axis_index("layer")

    def at(dr=0, dq=0, dl=0):
        return {
            "row": lax.rem(r + dr + n_row, n_row),
            "col": lax.rem(q + dq + n_col, n_col),
            "layer": lax.rem(l + dl + n_layer, n_layer),
        }

    counter = [0]

    def send(src, dst, target):
        i = counter[0]
        counter[0] += 1
        copy = pltpu.make_async_remote_copy(
            src_ref=src,
            dst_ref=dst,
            send_sem=send_sem.at[i],
            recv_sem=recv_sem.at[i],
            device_id=target,
            device_id_type=pl.DeviceIdType.MESH,
        )
        copy.start()
        sent.append(copy)
        return copy

    sent = []
    local_counter = [0]

    def local(src, dst):
        i = local_counter[0]
        local_counter[0] += 1
        copy = pltpu.make_async_copy(src, dst, local_sem.at[i])
        copy.start()
        return copy

    nt = nc // n_layer
    half = nt // 2

    own_a = [
        local(a_hbm.at[:, pl.ds(m * rows, rows), :], a_bufs[0][m].at[pl.ds(0, ta)]) for m in range(PARTS)
    ]
    own_b = local(b_hbm, b_buf)

    barrier = pltpu.get_barrier_semaphore()
    partners = [at(1, -1), at(-1, 1), at(0, 1), at(0, -1), at(0, 2), at(0, -2), at(0, 0, 1), at(0, 0, -1)]
    for partner in partners:
        pl.semaphore_signal(barrier, inc=1, device_id=partner, device_id_type=pl.DeviceIdType.MESH)
    pl.semaphore_wait(barrier, len(partners))

    next_a = at(1, -1)
    hop1 = [
        send(
            a_hbm.at[:, pl.ds(m * rows, rows), :],
            a_bufs[1][m].at[pl.ds(0, ta)],
            next_a,
        )
        for m in range(PARTS)
    ]

    def forward(m):
        hop1[m].wait_recv()
        return send(a_bufs[1][m].at[pl.ds(0, ta)], a_bufs[2][m].at[pl.ds(0, ta)], next_a)

    plan_copy = [None] * 3
    for s in range(3):
        listed = sort_lists(pairs_ref[s], lanes, ta, nc)
        for i, row in enumerate(listed):
            plan_out[s][pl.ds(i, 1), :] = row
        plan_out[s][pl.ds(6, 2), :] = jnp.zeros((2, lanes), jnp.int32)
        if s == 0:
            plan_copy[0] = local(plan_out[0], plan_s[0])
        else:
            plan_copy[s] = send(plan_out[s], plan_in[s - 1], at(0, -s))

    for s in range(3):
        for m in range(PARTS):
            a_bufs[s][m][ta] = jnp.zeros((rows, bs), a_bufs[s][m].dtype)
    products[0] = jnp.zeros((rows, bs), jnp.float32)

    def compute(s, m):
        a_buf, plan, target = a_bufs[s][m], plan_s[s], partial[s][m]

        def one(k, running):
            left = jnp.concatenate([a_buf[plan[0, k]], a_buf[plan[1, k]]], axis=1)
            right = jnp.concatenate([b_buf[plan[2, k]], b_buf[plan[3, k]]], axis=0)
            product = jnp.dot(left, right, preferred_element_type=jnp.float32)
            running = jnp.where(plan[4, k] > 0, running, 0.0) + product
            products[k + 1] = running
            return running

        lax.fori_loop(0, chunks, one, jnp.zeros((rows, bs), jnp.float32), unroll=unroll)
        for c in range(nc):
            target[c] = products[plan[5, c]]

    right, left, across = at(0, 0, 1), at(0, 0, -1), at(0, 0, 2)
    right_at, left_at, across_at = nt * right["layer"], nt * left["layer"], nt * across["layer"]
    far_copies, plain_copies, summed_copies, shift_copies = {}, {}, {}, {}

    def spread(s, m):
        source = partial[s][m]
        far_copies[s, m] = (
            send(source.at[pl.ds(across_at, half)], far_l[s][m], right),
            send(source.at[pl.ds(across_at + half, half)], far_r[s][m], left),
        )
        plain_copies[s, m] = (
            send(source.at[pl.ds(right_at + half, half)], near_l[s][m].at[pl.ds(half, half)], right),
            send(source.at[pl.ds(left_at, half)], near_r[s][m].at[pl.ds(0, half)], left),
        )

    def relay(s, m):
        source = partial[s][m]
        from_left, from_right = far_copies[s, m]
        from_left.wait_recv()
        source[pl.ds(right_at, half)] = source[pl.ds(right_at, half)] + far_l[s][m][...]
        one = send(source.at[pl.ds(right_at, half)], near_l[s][m].at[pl.ds(0, half)], right)
        from_right.wait_recv()
        source[pl.ds(left_at + half, half)] = source[pl.ds(left_at + half, half)] + far_r[s][m][...]
        two = send(source.at[pl.ds(left_at + half, half)], near_r[s][m].at[pl.ds(half, half)], left)
        summed_copies[s, m] = (one, two)

    def collect(s, m):
        for copy in plain_copies[s, m] + summed_copies[s, m]:
            copy.wait_recv()
        own = partial[s][m][pl.ds(nt * l, nt)]
        total[s][m][...] = own + near_l[s][m][...] + near_r[s][m][...]
        if s:
            shift_copies[s, m] = send(total[s][m], shift[s - 1][m], at(0, s))

    def finish(m):
        for s in (1, 2):
            shift_copies[s, m].wait_recv()
        out_ref[:, pl.ds(m * rows, rows), :] = total[0][m][...] + shift[0][m][...] + shift[1][m][...]

    hop2 = [None] * PARTS
    own_b.wait()
    for copy in own_a:
        copy.wait()
    plan_copy[0].wait()
    compute(0, 0)
    spread(0, 0)
    hop2[0] = forward(0)
    compute(0, 1)
    spread(0, 1)
    plan_copy[1].wait_recv()
    plan_1 = local(plan_in[0], plan_s[1])
    plan_copy[2].wait_recv()
    plan_2 = local(plan_in[1], plan_s[2])
    relay(0, 0)
    plan_1.wait()
    plan_2.wait()
    compute(1, 0)
    spread(1, 0)
    relay(0, 1)
    collect(0, 0)
    hop2[1] = forward(1)
    compute(1, 1)
    spread(1, 1)
    relay(1, 0)
    collect(0, 1)
    hop2[0].wait_recv()
    compute(2, 0)
    spread(2, 0)
    relay(1, 1)
    collect(1, 0)
    relay(2, 0)
    collect(1, 1)
    hop2[1].wait_recv()
    compute(2, 1)
    spread(2, 1)
    collect(2, 0)
    relay(2, 1)
    finish(0)
    collect(2, 1)
    finish(1)
    for copy in sent:
        copy.wait_send()


def shards(left_panels, right_panels, pair_lists):
    left_own = left_panels[0, 0, 0]
    right_own = right_panels[0, 0, 0]
    pairs = pair_lists[0, 0, 0]
    ta, bs, _ = left_own.shape
    tb = right_own.shape[0]
    slots = pairs.shape[2]
    nc = 16
    n_row, n_col, n_layer = (lax.axis_size(axis) for axis in ("row", "col", "layer"))
    nt = nc // n_layer
    rows = bs // PARTS
    chunks = (slots + nc) // 2
    lanes = slots
    unroll = UNROLL if chunks % UNROLL == 0 else 2
    f32, i32, bf16 = jnp.float32, jnp.int32, left_own.dtype
    vmem = pltpu.VMEM
    scratch = [vmem((ta + 1, rows, bs), bf16) for _ in range(3 * PARTS)]
    scratch += [vmem((tb, bs, bs), bf16), vmem((chunks + 1, rows, bs), f32)]
    scratch += [vmem((8, lanes), i32) for _ in range(5)]
    scratch += [pltpu.SMEM((8, lanes), i32) for _ in range(3)]
    scratch += [vmem((nc, rows, bs), f32) for _ in range(3 * PARTS)]
    scratch += [vmem((nt // 2, rows, bs), f32) for _ in range(6 * PARTS)]
    scratch += [vmem((nt, rows, bs), f32) for _ in range(11 * PARTS)]
    copies = 2 * PARTS + 2 + 18 * PARTS + 2 * PARTS
    scratch += [pltpu.SemaphoreType.DMA((PARTS + 4,))]
    scratch += [pltpu.SemaphoreType.DMA((copies,)), pltpu.SemaphoreType.DMA((copies,))]
    sizes = (n_row, n_col, n_layer, ta, bs, nc, chunks, lanes, unroll)
    tiles = pl.pallas_call(
        functools.partial(kernel, sizes=sizes),
        out_shape=jax.ShapeDtypeStruct((nt, bs, bs), f32),
        in_specs=[
            pl.BlockSpec(memory_space=pltpu.VMEM),
            pl.BlockSpec(memory_space=pl.ANY),
            pl.BlockSpec(memory_space=pl.ANY),
        ],
        out_specs=pl.BlockSpec(memory_space=pltpu.VMEM),
        scratch_shapes=scratch,
        compiler_params=pltpu.CompilerParams(
            collective_id=0, has_side_effects=True, vmem_limit_bytes=40 * 2**20
        ),
        cost_estimate=pl.CostEstimate(flops=3 * slots * 2 * bs**3, bytes_accessed=3 * 2**20, transcendentals=0),
    )(pairs, left_own, right_own)
    return tiles[None, None]


def solution(mesh):
    placed = (
        P("row", "col", "layer", None, None, None),
        P("row", "col", "layer", None, None, None),
        P("row", "col", "layer", None, None, None),
    )
    return jax.shard_map(
        shards,
        mesh=mesh,
        in_specs=placed,
        out_specs=P("row", "col", "layer", None, None),
        check_vma=False,
    )
```

profile of v0, /device:TPU:32, one launch (start us, length us, event | category | flops | bytes accessed | tf_op | source)
XLA Modules:
  0.0 64.6 jit_solution(10007361891532686238)
XLA Ops:
  0.0 0.7 %copy.6 = s32[1,1,1,3,3,256]{5,4,2,3,1,0:T(4,128)S(1)} copy(s32[1,1,1,3,3,256]{5,2,4,3,1,0:T(1,128)} %param.5) | data formatting | bytes 18432
  0.7 0.0 copy-start
  0.7 1.6 %copy-done = bf16[1,1,1,64,128,128]{5,4,3,2,1,0:T(8,128)(2,1)S(1)} copy-done((bf16[1,1,1,64,128,128]{5,4,3,2,1,0:T(8,128)(2,1)S(1)}, bf16[1,1,1,64,128,128]{5,4,3,2,1,0:T(8,128)(2,1)}, u32[]{:S(2)}) %copy-start) | copy-done | bytes 2097176
  2.3 0.0 copy-start.1
  2.3 1.0 %copy-done.1 = bf16[1,1,1,16,128,128]{5,4,3,2,1,0:T(8,128)(2,1)S(1)} copy-done((bf16[1,1,1,16,128,128]{5,4,3,2,1,0:T(8,128)(2,1)S(1)}, bf16[1,1,1,16,128,128]{5,4,3,2,1,0:T(8,128)(2,1)}, u32[]{:S(2)}) %copy-start.1) | copy-done | bytes 524312
  3.3 60.6 %shard_map.37 = f32[4,128,128]{2,1,0:T(8,128)S(1)} custom-call(s32[3,3,256]{2,1,0:T(4,128)S(1)} %bitcast.7, bf16[16,128,128]{2,1,0:T(8,128)(2,1)S(1)} %bitcast.9, bf16[64,128,128]{2,1,0:T(8,128)(2,1)S(1)} %bitcast.8), custom_call_target="tpu_custom_call" | custom-call | flops 3221225472 | bytes 3145728 | tf_op jit(solution)/shard_map/pallas_call | solution.py:289
  63.9 0.7 %copy.8 = f32[1,1,4,128,128]{4,3,2,1,0:T(8,128)} copy(f32[1,1,4,128,128]{4,3,2,1,0:T(8,128)S(1)} %bitcast.6) | data formatting | bytes 524288
Async XLA Ops:
  0.7 1.6 %copy-start = (bf16[1,1,1,64,128,128]{5,4,3,2,1,0:T(8,128)(2,1)S(1)}, bf16[1,1,1,64,128,128]{5,4,3,2,1,0:T(8,128)(2,1)}, u32[]{:S(2)}) copy-start(bf16[1,1,1,64,128,128]{5,4,3,2,1,0:T(8,128)(2,1)} %param.4) | copy-start | bytes 6291460
  2.3 1.0 %copy-start.1 = (bf16[1,1,1,16,128,128]{5,4,3,2,1,0:T(8,128)(2,1)S(1)}, bf16[1,1,1,16,128,128]{5,4,3,2,1,0:T(8,128)(2,1)}, u32[]{:S(2)}) copy-start(bf16[1,1,1,16,128,128]{5,4,3,2,1,0:T(8,128)(2,1)} %param.3) | copy-start | bytes 1572868
where the time goes:
time: 65.4 us; the launch traced here: 64.6 us
  Pallas kernels  60.6 us (93%)
  local copies, waits for them, and re-layouts  4.04 us (6%)
    pallas_call x1, Pallas kernels, shards(): pl.pallas_call(functools.partial(kernel, sizes=sizes), out_shape=jax.Shap...  60.6 us
    unnamed x6, local copies, waits for them, and re-layouts  4.04 us

commit v1 on v0

v1 whole, which is shorter than its diff:
```python
import functools

import jax
import jax.numpy as jnp
from jax import lax
from jax.experimental import pallas as pl
from jax.experimental.pallas import tpu as pltpu
from jax.sharding import PartitionSpec as P

PARTS = ((64, 64), (64, 32, 32), (32, 32, 16, 16, 16, 16))
PIECES = (32, 32, 16, 16, 16, 16)
UNROLL = {128: 68, 64: 68, 48: 68, 32: 68, 16: 68}
DIRECT = ("11", "12", "20", "21", "22", "23", "24", "25")
SCHEDULE = (
    "o0", "c00", "o1", "q", "s00", "f0", "o2", "c01", "s01", "o3", "p", "c10", "s10", "f1", "c20", "f2",
    "s20", "r10", "f3", "o4", "o5", "c11", "s11", "c21", "s21", "k20", "c22", "k10", "f4", "c23", "s22", "k11",
    "f5", "s23", "c12", "k21", "s12", "c24", "k22", "c25", "s25", "s24", "r00", "k23", "k12", "r01", "k25", "k24",
    "k00", "k01", "z10", "z12", "z23", "z20", "z25", "z11", "z21", "z22", "z24",
)


def sort_lists(pairs, chunk_lanes, zero_block, block_count):
    a_row, b_row, c_row = pairs
    slots = c_row.shape[1]
    iota = lambda shape, dim: lax.broadcasted_iota(jnp.int32, shape, dim)
    square = (slots, slots)
    c_across = jnp.broadcast_to(c_row, square)
    c_down = jnp.transpose(c_across)
    earlier = iota(square, 0) < iota(square, 1)
    rank = jnp.sum(jnp.where((c_down == c_across) & earlier, 1, 0), axis=0, keepdims=True)
    group = iota((block_count, slots), 0)
    c_short = jnp.broadcast_to(c_row, (block_count, slots))
    counts = jnp.sum(jnp.where(c_short == group, 1, 0), axis=1, keepdims=True)
    halves = jnp.broadcast_to((counts + 1) >> 1, (block_count, slots))
    before = jnp.sum(jnp.where(group < c_short, halves, 0), axis=0, keepdims=True)
    place = jnp.where(c_row < block_count, 2 * before + rank, 1023)
    first = jnp.where(rank == 0, 1, 0)
    word = place + (a_row << 10) + (b_row << 15) + (c_row << 22) + (first << 28)
    down = jnp.transpose(jnp.broadcast_to(word, square))
    if chunk_lanes != slots:
        down = down[:, :chunk_lanes]
    place = down & 1023
    entry = (((down >> 10) & 31) + 1) + (((down >> 15) & 127) << 8) + (((down >> 28) & 1) << 16)
    c_down = (down >> 22) & 63
    lane = iota((slots, chunk_lanes), 1)
    one = jnp.sum(jnp.where(place == 2 * lane, entry, 0), axis=0, keepdims=True)
    two = jnp.sum(jnp.where(place == 2 * lane + 1, entry, 0), axis=0, keepdims=True)
    last = jnp.max(jnp.where((c_down == lane) & (place < 1023), (place >> 1) + 1, 0), axis=0, keepdims=True)
    rows = []
    for picked in (one, two):
        a = picked & 255
        rows.append(jnp.where(a == 0, zero_block, a - 1))
    for picked in (one, two):
        rows.append((picked >> 8) & 255)
    rows.append(1 - ((one >> 16) & 1))
    rows.append(last)
    return rows


def kernel(pairs_hbm, a_hbm, b_hbm, out_ref, *scratch, sizes):
    n_row, n_col, n_layer, ta, bs, nc, chunks, lanes, parts, pieces, unroll = sizes
    steps = len(parts)
    starts = lambda heights: [sum(heights[:m]) for m in range(len(heights))]
    offsets = [starts(heights) for heights in parts]
    piece_offsets = starts(pieces)
    scratch = list(scratch)

    def take(count):
        taken = scratch[:count]
        del scratch[:count]
        return taken

    def take_parts():
        return [take(len(heights)) for heights in parts]

    a_bufs = take_parts()
    b_buf, pairs_ref = take(2)
    heights_used = sorted({rows for heights in parts for rows in heights})
    products = dict(zip(heights_used, take(len(heights_used))))
    plan_out = take(steps)
    plan_in = take(steps - 1)
    plan_s = take(steps)
    partial, far, near_l, near_r, total, shift = (take_parts() for _ in range(6))
    local_sem, send_sem, recv_sem = take(3)

    r, q, l = lax.axis_index("row"), lax.axis_index("col"), lax.axis_index("layer")

    def at(dr=0, dq=0, dl=0):
        return {
            "row": lax.rem(r + dr + n_row, n_row),
            "col": lax.rem(q + dq + n_col, n_col),
            "layer": lax.rem(l + dl + n_layer, n_layer),
        }

    sent, started = [], []

    def send(src, dst, target):
        i = len(sent)
        copy = pltpu.make_async_remote_copy(
            src_ref=src,
            dst_ref=dst,
            send_sem=send_sem.at[i],
            recv_sem=recv_sem.at[i],
            device_id=target,
            device_id_type=pl.DeviceIdType.MESH,
        )
        copy.start()
        sent.append(copy)
        return copy

    def local(src, dst):
        copy = pltpu.make_async_copy(src, dst, local_sem.at[len(started)])
        copy.start()
        started.append(copy)
        return copy

    arrived = set()

    def arrive(copy):
        if id(copy) not in arrived:
            arrived.add(id(copy))
            copy.wait_recv()

    nt = nc // n_layer
    half = nt // 2

    own_pairs = local(pairs_hbm, pairs_ref)
    own_a = [
        local(a_hbm.at[:, pl.ds(offset, rows), :], buf.at[pl.ds(0, ta)])
        for offset, rows, buf in zip(offsets[0], parts[0], a_bufs[0])
    ]
    own_b = local(b_hbm, b_buf)

    barrier = pltpu.get_barrier_semaphore()
    partners = [at(1, -1), at(-1, 1), at(0, 1), at(0, -1), at(0, 2), at(0, -2)]
    partners += [at(0, 0, 1), at(0, 0, -1), at(0, 0, 2)]
    for partner in partners:
        pl.semaphore_signal(barrier, inc=1, device_id=partner, device_id_type=pl.DeviceIdType.MESH)
    pl.semaphore_wait(barrier, len(partners))

    next_a = at(1, -1)
    hop1, hop2 = {}, {}

    def members(s, m):
        low, high = offsets[s][m], offsets[s][m] + parts[s][m]
        return [i for i, offset in enumerate(piece_offsets) if low <= offset < high]

    def piece_of(s, i):
        for m in range(len(parts[s])):
            if i in members(s, m):
                return a_bufs[s][m].at[pl.ds(0, ta), pl.ds(piece_offsets[i] - offsets[s][m], pieces[i])]

    def begin(i):
        source = a_hbm.at[:, pl.ds(piece_offsets[i], pieces[i]), :]
        hop1[i] = send(source, piece_of(1, i), next_a)

    def forward(i):
        arrive(hop1[i])
        hop2[i] = send(piece_of(1, i), piece_of(2, i), next_a)

    order = list(SCHEDULE)
    while order[0][0] == "o":
        begin(int(order.pop(0)[1]))

    plan_copy = {}

    def list_step(s):
        listed = sort_lists([pairs_ref[s, i] for i in range(3)], lanes, ta, nc)
        for i, row in enumerate(listed):
            plan_out[s][pl.ds(i, 1), :] = row
        plan_out[s][pl.ds(6, 2), :] = jnp.zeros((2, lanes), jnp.int32)
        if s == 0:
            plan_copy[s] = local(plan_out[0], plan_s[0])
        else:
            plan_copy[s] = send(plan_out[s], plan_in[s - 1], at(0, -s))

    own_pairs.wait()
    list_step(0)

    for bufs in a_bufs:
        for buf in bufs:
            buf[ta] = jnp.zeros(buf.shape[1:], buf.dtype)
    for buf in products.values():
        buf[0] = jnp.zeros(buf.shape[1:], buf.dtype)

    def send_plans():
        for s in range(1, steps):
            list_step(s)

    def plans():
        for i in range(1, steps):
            arrive(plan_copy[i])
            plan_copy[i] = local(plan_in[i - 1], plan_s[i])

    waited = set()

    def once(copy):
        if id(copy) not in waited:
            waited.add(id(copy))
            copy.wait()

    def compute(s, m):
        once(plan_copy[s])
        if s == 0:
            once(own_b)
            once(own_a[m])
        else:
            for i in members(s, m):
                arrive((hop1, hop2)[s - 1][i])
        rows = parts[s][m]
        a_buf, plan, target, running_sums = a_bufs[s][m], plan_s[s], partial[s][m], products[rows]

        def one(k, running):
            left = jnp.concatenate([a_buf[plan[0, k]], a_buf[plan[1, k]]], axis=1)
            right = jnp.concatenate([b_buf[plan[2, k]], b_buf[plan[3, k]]], axis=0)
            product = jnp.dot(left, right, preferred_element_type=jnp.float32)
            running = jnp.where(plan[4, k] > 0, running, 0.0) + product
            running_sums[k + 1] = running
            return running

        lax.fori_loop(0, chunks, one, jnp.zeros((rows, bs), jnp.float32), unroll=unroll[rows])
        for c in range(nc):
            target[c] = running_sums[plan[5, c]]

    right, left, across = at(0, 0, 1), at(0, 0, -1), at(0, 0, 2)
    right_at, left_at, across_at = nt * right["layer"], nt * left["layer"], nt * across["layer"]
    far_copies, plain_copies, summed_copies, shift_copies = {}, {}, {}, {}

    def is_direct(s, m):
        return f"{s}{m}" in DIRECT

    def spread(s, m):
        source = partial[s][m]
        if is_direct(s, m):
            plain_copies[s, m] = (
                send(source.at[pl.ds(across_at, nt)], far[s][m], across),
                send(source.at[pl.ds(right_at, nt)], near_l[s][m], right),
                send(source.at[pl.ds(left_at, nt)], near_r[s][m], left),
            )
            return
        far_copies[s, m] = (
            send(source.at[pl.ds(across_at, half)], far[s][m].at[pl.ds(0, half)], right),
            send(source.at[pl.ds(across_at + half, half)], far[s][m].at[pl.ds(half, half)], left),
        )
        plain_copies[s, m] = (
            send(source.at[pl.ds(right_at + half, half)], near_l[s][m].at[pl.ds(half, half)], right),
            send(source.at[pl.ds(left_at, half)], near_r[s][m].at[pl.ds(0, half)], left),
        )

    def relay(s, m):
        source, passed = partial[s][m], far[s][m]
        from_left, from_right = far_copies[s, m]
        arrive(from_left)
        source[pl.ds(right_at, half)] = source[pl.ds(right_at, half)] + passed[pl.ds(0, half)]
        one = send(source.at[pl.ds(right_at, half)], near_l[s][m].at[pl.ds(0, half)], right)
        arrive(from_right)
        source[pl.ds(left_at + half, half)] = source[pl.ds(left_at + half, half)] + passed[pl.ds(half, half)]
        two = send(source.at[pl.ds(left_at + half, half)], near_r[s][m].at[pl.ds(half, half)], left)
        summed_copies[s, m] = (one, two)

    def collect(s, m):
        for copy in plain_copies[s, m] + summed_copies.get((s, m), ()):
            arrive(copy)
        summed = partial[s][m][pl.ds(nt * l, nt)] + near_l[s][m][...] + near_r[s][m][...]
        if is_direct(s, m):
            summed = summed + far[s][m][...]
        if s == 0:
            out_ref[:, pl.ds(offsets[s][m], parts[s][m]), :] = summed
        else:
            total[s][m][...] = summed
            shift_copies[s, m] = send(total[s][m], shift[s][m], at(0, s))

    def finish(s, m):
        arrive(shift_copies[s, m])
        rows = pl.ds(offsets[s][m], parts[s][m])
        out_ref[:, rows, :] = out_ref[:, rows, :] + shift[s][m][...]

    actions = {
        "o": begin,
        "f": forward,
        "c": compute,
        "s": spread,
        "r": relay,
        "k": collect,
        "z": finish,
        "p": plans,
        "q": send_plans,
    }
    for step in order:
        actions[step[0]](*(int(digit) for digit in step[1:]))
    for copy in sent:
        copy.wait_send()


def shards(left_panels, right_panels, pair_lists):
    left_own = left_panels[0, 0, 0]
    right_own = right_panels[0, 0, 0]
    pairs = pair_lists[0, 0, 0][:, :, None, :]
    ta, bs, _ = left_own.shape
    tb = right_own.shape[0]
    steps, _, _, slots = pairs.shape
    nc = 16
    n_row, n_col, n_layer = (lax.axis_size(axis) for axis in ("row", "col", "layer"))
    nt = nc // n_layer
    parts = tuple(tuple(rows * bs // 128 for rows in heights) for heights in PARTS)
    pieces = tuple(rows * bs // 128 for rows in PIECES)
    chunks = (slots + nc) // 2
    unroll = {rows * bs // 128: by if chunks % by == 0 else 2 for rows, by in UNROLL.items()}
    f32, i32, bf16 = jnp.float32, jnp.int32, left_own.dtype
    vmem = pltpu.VMEM
    every = [rows for heights in parts for rows in heights]
    scratch = [vmem((ta + 1, rows, bs), bf16) for rows in every]
    scratch += [vmem((tb, bs, bs), bf16), vmem(pairs.shape, i32)]
    scratch += [vmem((chunks + 1, rows, bs), f32) for rows in sorted(set(every))]
    scratch += [vmem((8, slots), i32) for _ in range(2 * steps - 1)]
    scratch += [pltpu.SMEM((8, slots), i32) for _ in range(steps)]
    for blocks in (nc, nt, nt, nt, nt, nt):
        scratch += [vmem((blocks, rows, bs), f32) for rows in every]
    copies = 2 * len(pieces) + 2 + 7 * len(every)
    scratch += [pltpu.SemaphoreType.DMA((len(parts[0]) + 5,))]
    scratch += [pltpu.SemaphoreType.DMA((copies,)), pltpu.SemaphoreType.DMA((copies,))]
    sizes = (n_row, n_col, n_layer, ta, bs, nc, chunks, slots, parts, pieces, unroll)
    tiles = pl.pallas_call(
        functools.partial(kernel, sizes=sizes),
        out_shape=jax.ShapeDtypeStruct((nt, bs, bs), f32),
        in_specs=[
            pl.BlockSpec(memory_space=pltpu.HBM),
            pl.BlockSpec(memory_space=pltpu.HBM),
            pl.BlockSpec(memory_space=pltpu.HBM),
        ],
        out_specs=pl.BlockSpec(memory_space=pltpu.VMEM),
        scratch_shapes=scratch,
        compiler_params=pltpu.CompilerParams(
            collective_id=0, has_side_effects=True, vmem_limit_bytes=50 * 2**20
        ),
        cost_estimate=pl.CostEstimate(flops=3 * slots * 2 * bs**3, bytes_accessed=3 * 2**20, transcendentals=0),
    )(*(pltpu.with_memory_space_constraint(x, pltpu.HBM) for x in (pairs, left_own, right_own)))
    return tiles[None, None]


def solution(mesh):
    placed = (
        P("row", "col", "layer", None, None, None),
        P("row", "col", "layer", None, None, None),
        P("row", "col", "layer", None, None, None),
    )
    return jax.shard_map(
        shards,
        mesh=mesh,
        in_specs=placed,
        out_specs=P("row", "col", "layer", None, None),
        check_vma=False,
    )
```

time: 65.4 us -> 53.2 us (0.81); the launches traced: 64.6 us -> 53.1 us
  Pallas kernels: 60.6 us -> 52.4 us
  local copies, waits for them, and re-layouts: 4.04 us -> 0.71 us
    pallas_call x1, Pallas kernels: 60.6 us -> 52.4 us  [shards(): pl.pallas_call(functools.partial(kernel, sizes=sizes), out_shape=jax.Shap...]
    unnamed x6 -> x1, local copies, waits for them, and re-layouts: 4.04 us -> 0.71 us
where the time goes in v1:
time: 53.2 us; the launch traced here: 53.1 us
  Pallas kernels  52.4 us (98%)
  local copies, waits for them, and re-layouts  0.71 us (1%)
    pallas_call x1, Pallas kernels, shards(): pl.pallas_call(functools.partial(kernel, sizes=sizes), out_shape=jax.Shap...  52.4 us

profile of v1, /device:TPU:32, one launch (start us, length us, event | category | flops | bytes accessed | tf_op | source)
XLA Modules:
  0.0 53.1 jit_solution(4572752388228565484)
XLA Ops:
  0.0 52.4 %shard_map.37 = f32[4,128,128]{2,1,0:T(8,128)S(1)} custom-call(s32[3,3,1,256]{3,2,1,0:T(1,128)} %bitcast.7, bf16[16,128,128]{2,1,0:T(8,128)(2,1)} %bitcast.6, bf16[64,128,128]{2,1,0:T(8,128)(2,1)} %bitcast.5), custom_call_target="tpu_custom_call" | custom-call | flops 3221225472 | bytes 3145728 | tf_op jit(solution)/shard_map/pallas_call | solution.py:323
  52.4 0.7 %copy.5 = f32[1,1,4,128,128]{4,3,2,1,0:T(8,128)} copy(f32[1,1,4,128,128]{4,3,2,1,0:T(8,128)S(1)} %bitcast.4) | data formatting | bytes 524288

commit v2 on v1

--- a/solution.py
+++ b/solution.py
@@ -80,7 +80,7 @@
     plan_out = take(steps)
     plan_in = take(steps - 1)
     plan_s = take(steps)
-    partial, far, near_l, near_r, total, shift = (take_parts() for _ in range(6))
+    partial, inbox, total, shift = (take_parts() for _ in range(4))
     local_sem, send_sem, recv_sem = take(3)
 
     r, q, l = lax.axis_index("row"), lax.axis_index("col"), lax.axis_index("layer")
@@ -92,21 +92,29 @@
             "layer": lax.rem(l + dl + n_layer, n_layer),
         }
 
-    sent, started = [], []
-
-    def send(src, dst, target):
-        i = len(sent)
+    started = []
+    send_slots, recv_slots = {}, {}
+
+    def send_slot(key):
+        return send_sem.at[send_slots.setdefault(key, len(send_slots))]
+
+    def recv_slot(key):
+        return recv_sem.at[recv_slots.setdefault(key, len(recv_slots))]
+
+    def send(src, dst, target, send_key, recv_key):
         copy = pltpu.make_async_remote_copy(
             src_ref=src,
             dst_ref=dst,
-            send_sem=send_sem.at[i],
-            recv_sem=recv_sem.at[i],
+            send_sem=send_slot(send_key),
+            recv_sem=recv_slot(recv_key),
             device_id=target,
             device_id_type=pl.DeviceIdType.MESH,
         )
         copy.start()
-        sent.append(copy)
         return copy
+
+    def wait_bytes(ref, sem):
+        pltpu.make_async_copy(ref, ref, sem).wait()
 
     def local(src, dst):
         copy = pltpu.make_async_copy(src, dst, local_sem.at[len(started)])
@@ -124,6 +132,11 @@
     nt = nc // n_layer
     half = nt // 2
 
+    barrier = pltpu.get_barrier_semaphore()
+    partners = [at(0, 2), at(0, -2), at(-1, 1), at(1, -1), at(0, 1), at(0, -1)]
+    partners += [at(0, 0, 1), at(0, 0, -1), at(0, 0, 2)]
+    for partner in partners:
+        pl.semaphore_signal(barrier, inc=1, device_id=partner, device_id_type=pl.DeviceIdType.MESH)
     own_pairs = local(pairs_hbm, pairs_ref)
     own_a = [
         local(a_hbm.at[:, pl.ds(offset, rows), :], buf.at[pl.ds(0, ta)])
@@ -131,15 +144,17 @@
     ]
     own_b = local(b_hbm, b_buf)
 
-    barrier = pltpu.get_barrier_semaphore()
-    partners = [at(1, -1), at(-1, 1), at(0, 1), at(0, -1), at(0, 2), at(0, -2)]
-    partners += [at(0, 0, 1), at(0, 0, -1), at(0, 0, 2)]
-    for partner in partners:
-        pl.semaphore_signal(barrier, inc=1, device_id=partner, device_id_type=pl.DeviceIdType.MESH)
     pl.semaphore_wait(barrier, len(partners))
 
     next_a = at(1, -1)
     hop1, hop2 = {}, {}
+
+    waited = set()
+
+    def once(copy):
+        if id(copy) not in waited:
+            waited.add(id(copy))
+            copy.wait()
 
     def members(s, m):
         low, high = offsets[s][m], offsets[s][m] + parts[s][m]
@@ -151,12 +166,14 @@
                 return a_bufs[s][m].at[pl.ds(0, ta), pl.ds(piece_offsets[i] - offsets[s][m], pieces[i])]
 
     def begin(i):
-        source = a_hbm.at[:, pl.ds(piece_offsets[i], pieces[i]), :]
-        hop1[i] = send(source, piece_of(1, i), next_a)
+        for m, offset in enumerate(offsets[0]):
+            if offset <= piece_offsets[i] < offset + parts[0][m]:
+                once(own_a[m])
+        hop1[i] = send(piece_of(0, i), piece_of(1, i), next_a, "own", ("first", i))
 
     def forward(i):
         arrive(hop1[i])
-        hop2[i] = send(piece_of(1, i), piece_of(2, i), next_a)
+        hop2[i] = send(piece_of(1, i), piece_of(2, i), next_a, "passed", ("second", i))
 
     order = list(SCHEDULE)
     while order[0][0] == "o":
@@ -172,7 +189,7 @@
         if s == 0:
             plan_copy[s] = local(plan_out[0], plan_s[0])
         else:
-            plan_copy[s] = send(plan_out[s], plan_in[s - 1], at(0, -s))
+            plan_copy[s] = send(plan_out[s], plan_in[s - 1], at(0, -s), ("plan", s), ("plan", s))
 
     own_pairs.wait()
     list_step(0)
@@ -187,17 +204,13 @@
         for s in range(1, steps):
             list_step(s)
 
+    plan_sends = []
+
     def plans():
         for i in range(1, steps):
             arrive(plan_copy[i])
+            plan_sends.append(plan_copy[i])
             plan_copy[i] = local(plan_in[i - 1], plan_s[i])
-
-    waited = set()
-
-    def once(copy):
-        if id(copy) not in waited:
-            waited.add(id(copy))
-            copy.wait()
 
     def compute(s, m):
         once(plan_copy[s])
@@ -224,51 +237,49 @@
 
     right, left, across = at(0, 0, 1), at(0, 0, -1), at(0, 0, 2)
     right_at, left_at, across_at = nt * right["layer"], nt * left["layer"], nt * across["layer"]
-    far_copies, plain_copies, summed_copies, shift_copies = {}, {}, {}, {}
+    shift_copies = {}
 
     def is_direct(s, m):
         return f"{s}{m}" in DIRECT
 
     def spread(s, m):
-        source = partial[s][m]
+        source, box = partial[s][m], inbox[s][m]
+
+        def pass_on(start, count, slot, target, kind="all"):
+            send(source.at[pl.ds(start, count)], box.at[pl.ds(slot, count)], target, (s, m), (kind, s, m))
+
         if is_direct(s, m):
-            plain_copies[s, m] = (
-                send(source.at[pl.ds(across_at, nt)], far[s][m], across),
-                send(source.at[pl.ds(right_at, nt)], near_l[s][m], right),
-                send(source.at[pl.ds(left_at, nt)], near_r[s][m], left),
-            )
+            pass_on(across_at, nt, 0, across)
+            pass_on(right_at, nt, nt, right)
+            pass_on(left_at, nt, 2 * nt, left)
             return
-        far_copies[s, m] = (
-            send(source.at[pl.ds(across_at, half)], far[s][m].at[pl.ds(0, half)], right),
-            send(source.at[pl.ds(across_at + half, half)], far[s][m].at[pl.ds(half, half)], left),
-        )
-        plain_copies[s, m] = (
-            send(source.at[pl.ds(right_at + half, half)], near_l[s][m].at[pl.ds(half, half)], right),
-            send(source.at[pl.ds(left_at, half)], near_r[s][m].at[pl.ds(0, half)], left),
-        )
+        pass_on(across_at, half, 0, right, "far")
+        pass_on(across_at + half, half, half, left, "far")
+        pass_on(right_at + half, half, nt + half, right)
+        pass_on(left_at, half, 2 * nt, left)
 
     def relay(s, m):
-        source, passed = partial[s][m], far[s][m]
-        from_left, from_right = far_copies[s, m]
-        arrive(from_left)
-        source[pl.ds(right_at, half)] = source[pl.ds(right_at, half)] + passed[pl.ds(0, half)]
-        one = send(source.at[pl.ds(right_at, half)], near_l[s][m].at[pl.ds(0, half)], right)
-        arrive(from_right)
-        source[pl.ds(left_at + half, half)] = source[pl.ds(left_at + half, half)] + passed[pl.ds(half, half)]
-        two = send(source.at[pl.ds(left_at + half, half)], near_r[s][m].at[pl.ds(half, half)], left)
-        summed_copies[s, m] = (one, two)
+        source, box = partial[s][m], inbox[s][m]
+        wait_bytes(box.at[pl.ds(0, nt)], recv_slot(("far", s, m)))
+        for start, slot, place, target in ((right_at, 0, nt, right), (left_at + half, half, 2 * nt + half, left)):
+            blocks = pl.ds(start, half)
+            source[blocks] = source[blocks] + box[pl.ds(slot, half)]
+            send(source.at[blocks], box.at[pl.ds(place, half)], target, (s, m), ("all", s, m))
 
     def collect(s, m):
-        for copy in plain_copies[s, m] + summed_copies.get((s, m), ()):
-            arrive(copy)
-        summed = partial[s][m][pl.ds(nt * l, nt)] + near_l[s][m][...] + near_r[s][m][...]
+        box, sem = inbox[s][m], recv_slot(("all", s, m))
+        summed = partial[s][m][pl.ds(nt * l, nt)]
         if is_direct(s, m):
-            summed = summed + far[s][m][...]
+            wait_bytes(box, sem)
+            summed = summed + box[pl.ds(0, nt)]
+        else:
+            wait_bytes(box.at[pl.ds(nt, 2 * nt)], sem)
+        summed = summed + box[pl.ds(nt, nt)] + box[pl.ds(2 * nt, nt)]
         if s == 0:
             out_ref[:, pl.ds(offsets[s][m], parts[s][m]), :] = summed
         else:
             total[s][m][...] = summed
-            shift_copies[s, m] = send(total[s][m], shift[s][m], at(0, s))
+            shift_copies[s, m] = send(total[s][m], shift[s][m], at(0, s), (s, m), ("shift", s, m))
 
     def finish(s, m):
         arrive(shift_copies[s, m])
@@ -288,7 +299,12 @@
     }
     for step in order:
         actions[step[0]](*(int(digit) for digit in step[1:]))
-    for copy in sent:
+    for s in range(steps):
+        for m, source in enumerate(partial[s]):
+            wait_bytes(source.at[pl.ds(0, 3 * nt + (nt if s else 0))], send_slot((s, m)))
+    for key in ("own", "passed"):
+        wait_bytes(b_buf.at[pl.ds(0, ta)], send_slot(key))
+    for copy in plan_sends:
         copy.wait_send()
 
 
@@ -314,11 +330,12 @@
     scratch += [vmem((chunks + 1, rows, bs), f32) for rows in sorted(set(every))]
     scratch += [vmem((8, slots), i32) for _ in range(2 * steps - 1)]
     scratch += [pltpu.SMEM((8, slots), i32) for _ in range(steps)]
-    for blocks in (nc, nt, nt, nt, nt, nt):
+    for blocks in (nc, 3 * nt, nt, nt):
         scratch += [vmem((blocks, rows, bs), f32) for rows in every]
-    copies = 2 * len(pieces) + 2 + 7 * len(every)
-    scratch += [pltpu.SemaphoreType.DMA((len(parts[0]) + 5,))]
-    scratch += [pltpu.SemaphoreType.DMA((copies,)), pltpu.SemaphoreType.DMA((copies,))]
+    sends = len(every) + 2 + steps - 1
+    receives = 2 * len(pieces) + steps - 1 + 3 * len(every) - len(DIRECT) - len(parts[0])
+    scratch += [pltpu.SemaphoreType.DMA((len(parts[0]) + steps + 2,))]
+    scratch += [pltpu.SemaphoreType.DMA((sends,)), pltpu.SemaphoreType.DMA((receives,))]
     sizes = (n_row, n_col, n_layer, ta, bs, nc, chunks, slots, parts, pieces, unroll)
     tiles = pl.pallas_call(
         functools.partial(kernel, sizes=sizes),

time: 53.2 us -> 51.6 us (0.970)
  Pallas kernels: 52.4 us -> 50.8 us
    pallas_call x1, Pallas kernels: 52.4 us -> 50.8 us  [shards(): pl.pallas_call(functools.partial(kernel, sizes=sizes), out_shape=jax.Shap...]
where the time goes in v2:
time: 51.6 us; the launch traced here: 51.5 us
  Pallas kernels  50.8 us (98%)
  local copies, waits for them, and re-layouts  0.71 us (1%)
    pallas_call x1, Pallas kernels, shards(): pl.pallas_call(functools.partial(kernel, sizes=sizes), out_shape=jax.Shap...  50.8 us

profile of v2, /device:TPU:32, one launch (start us, length us, event | category | flops | bytes accessed | tf_op | source)
XLA Modules:
  0.0 51.5 jit_solution(15305203248085034502)
XLA Ops:
  0.0 50.8 %shard_map.37 = f32[4,128,128]{2,1,0:T(8,128)S(1)} custom-call(s32[3,3,1,256]{3,2,1,0:T(1,128)} %bitcast.7, bf16[16,128,128]{2,1,0:T(8,128)(2,1)} %bitcast.6, bf16[64,128,128]{2,1,0:T(8,128)(2,1)} %bitcast.5), custom_call_target="tpu_custom_call" | custom-call | flops 3221225472 | bytes 3145728 | tf_op jit(solution)/shard_map/pallas_call | solution.py:340
  50.8 0.7 %copy.5 = f32[1,1,4,128,128]{4,3,2,1,0:T(8,128)} copy(f32[1,1,4,128,128]{4,3,2,1,0:T(8,128)S(1)} %bitcast.4) | data formatting | bytes 524288

commit v3 on v2

--- a/solution.py
+++ b/solution.py
@@ -12,10 +12,10 @@
 UNROLL = {128: 68, 64: 68, 48: 68, 32: 68, 16: 68}
 DIRECT = ("11", "12", "20", "21", "22", "23", "24", "25")
 SCHEDULE = (
-    "o0", "c00", "o1", "q", "s00", "f0", "o2", "c01", "s01", "o3", "p", "c10", "s10", "f1", "c20", "f2",
-    "s20", "r10", "f3", "o4", "o5", "c11", "s11", "c21", "s21", "k20", "c22", "k10", "f4", "c23", "s22", "k11",
-    "f5", "s23", "c12", "k21", "s12", "c24", "k22", "c25", "s25", "s24", "r00", "k23", "k12", "r01", "k25", "k24",
-    "k00", "k01", "z10", "z12", "z23", "z20", "z25", "z11", "z21", "z22", "z24",
+    "o0", "c00", "o1", "q", "s00", "c01", "f0", "s01", "o2", "o3", "p", "c10", "s10", "f1", "c20", "s20",
+    "f2", "o4", "f3", "o5", "r10", "c11", "s11", "c21", "k20", "s21", "c22", "f4", "s22", "k10", "c23", "f5",
+    "k11", "s23", "c12", "k21", "s12", "c24", "k22", "s24", "k23", "c25", "s25", "r00", "k12", "r01", "k24", "k25",
+    "k00", "k01", "z21", "z12", "z24", "z20", "z23", "z11", "z22", "z10", "z25",
 )
 
 
@@ -169,11 +169,11 @@
         for m, offset in enumerate(offsets[0]):
             if offset <= piece_offsets[i] < offset + parts[0][m]:
                 once(own_a[m])
-        hop1[i] = send(piece_of(0, i), piece_of(1, i), next_a, "own", ("first", i))
+        hop1[i] = send(piece_of(0, i), piece_of(1, i), next_a, "a", ("first", i))
 
     def forward(i):
         arrive(hop1[i])
-        hop2[i] = send(piece_of(1, i), piece_of(2, i), next_a, "passed", ("second", i))
+        hop2[i] = send(piece_of(1, i), piece_of(2, i), next_a, "a", ("second", i))
 
     order = list(SCHEDULE)
     while order[0][0] == "o":
@@ -246,7 +246,7 @@
         source, box = partial[s][m], inbox[s][m]
 
         def pass_on(start, count, slot, target, kind="all"):
-            send(source.at[pl.ds(start, count)], box.at[pl.ds(slot, count)], target, (s, m), (kind, s, m))
+            send(source.at[pl.ds(start, count)], box.at[pl.ds(slot, count)], target, s, (kind, s, m))
 
         if is_direct(s, m):
             pass_on(across_at, nt, 0, across)
@@ -264,7 +264,7 @@
         for start, slot, place, target in ((right_at, 0, nt, right), (left_at + half, half, 2 * nt + half, left)):
             blocks = pl.ds(start, half)
             source[blocks] = source[blocks] + box[pl.ds(slot, half)]
-            send(source.at[blocks], box.at[pl.ds(place, half)], target, (s, m), ("all", s, m))
+            send(source.at[blocks], box.at[pl.ds(place, half)], target, s, ("all", s, m))
 
     def collect(s, m):
         box, sem = inbox[s][m], recv_slot(("all", s, m))
@@ -279,7 +279,7 @@
             out_ref[:, pl.ds(offsets[s][m], parts[s][m]), :] = summed
         else:
             total[s][m][...] = summed
-            shift_copies[s, m] = send(total[s][m], shift[s][m], at(0, s), (s, m), ("shift", s, m))
+            shift_copies[s, m] = send(total[s][m], shift[s][m], at(0, s), s, ("shift", s, m))
 
     def finish(s, m):
         arrive(shift_copies[s, m])
@@ -300,10 +300,9 @@
     for step in order:
         actions[step[0]](*(int(digit) for digit in step[1:]))
     for s in range(steps):
-        for m, source in enumerate(partial[s]):
-            wait_bytes(source.at[pl.ds(0, 3 * nt + (nt if s else 0))], send_slot((s, m)))
-    for key in ("own", "passed"):
-        wait_bytes(b_buf.at[pl.ds(0, ta)], send_slot(key))
+        blocks = 3 * nt + (nt if s else 0)
+        wait_bytes(b_buf.at[pl.ds(0, 2 * blocks)], send_slot(s))
+    wait_bytes(b_buf.at[pl.ds(0, 2 * ta)], send_slot("a"))
     for copy in plan_sends:
         copy.wait_send()
 
@@ -332,7 +331,7 @@
     scratch += [pltpu.SMEM((8, slots), i32) for _ in range(steps)]
     for blocks in (nc, 3 * nt, nt, nt):
         scratch += [vmem((blocks, rows, bs), f32) for rows in every]
-    sends = len(every) + 2 + steps - 1
+    sends = steps + 1 + steps - 1
     receives = 2 * len(pieces) + steps - 1 + 3 * len(every) - len(DIRECT) - len(parts[0])
     scratch += [pltpu.SemaphoreType.DMA((len(parts[0]) + steps + 2,))]
     scratch += [pltpu.SemaphoreType.DMA((sends,)), pltpu.SemaphoreType.DMA((receives,))]

time: 51.6 us -> 51.3 us (level)
  no operation moved by 1% of the time
where the time goes in v3:
time: 51.3 us
  Pallas kernels  50.5 us (98%)
  local copies, waits for them, and re-layouts  0.71 us (1%)
    pallas_call x1, Pallas kernels, shards(): pl.pallas_call(functools.partial(kernel, sizes=sizes), out_shape=jax.Shap...  50.5 us

profile of v3, /device:TPU:32, one launch (start us, length us, event | category | flops | bytes accessed | tf_op | source)
XLA Modules:
  0.0 51.3 jit_solution(14961371584580239537)
XLA Ops:
  0.0 50.5 %shard_map.37 = f32[4,128,128]{2,1,0:T(8,128)S(1)} custom-call(s32[3,3,1,256]{3,2,1,0:T(1,128)} %bitcast.7, bf16[16,128,128]{2,1,0:T(8,128)(2,1)} %bitcast.6, bf16[64,128,128]{2,1,0:T(8,128)(2,1)} %bitcast.5), custom_call_target="tpu_custom_call" | custom-call | flops 3221225472 | bytes 3145728 | tf_op jit(solution)/shard_map/pallas_call | solution.py:339
  50.6 0.7 %copy.5 = f32[1,1,4,128,128]{4,3,2,1,0:T(8,128)} copy(f32[1,1,4,128,128]{4,3,2,1,0:T(8,128)S(1)} %bitcast.4) | data formatting | bytes 524288

commit v4 on v3

--- a/solution.py
+++ b/solution.py
@@ -279,10 +279,12 @@
             out_ref[:, pl.ds(offsets[s][m], parts[s][m]), :] = summed
         else:
             total[s][m][...] = summed
-            shift_copies[s, m] = send(total[s][m], shift[s][m], at(0, s), s, ("shift", s, m))
+            shift_copies[s, m] = send(total[s][m], shift[s][m], at(0, s), s, ("shift", s))
 
     def finish(s, m):
-        arrive(shift_copies[s, m])
+        if s not in arrived:
+            arrived.add(s)
+            wait_bytes(b_buf.at[pl.ds(0, 2 * nt)], recv_slot(("shift", s)))
         rows = pl.ds(offsets[s][m], parts[s][m])
         out_ref[:, rows, :] = out_ref[:, rows, :] + shift[s][m][...]
 
@@ -332,7 +334,7 @@
     for blocks in (nc, 3 * nt, nt, nt):
         scratch += [vmem((blocks, rows, bs), f32) for rows in every]
     sends = steps + 1 + steps - 1
-    receives = 2 * len(pieces) + steps - 1 + 3 * len(every) - len(DIRECT) - len(parts[0])
+    receives = 2 * len(pieces) + 2 * (steps - 1) + 2 * len(every) - len(DIRECT)
     scratch += [pltpu.SemaphoreType.DMA((len(parts[0]) + steps + 2,))]
     scratch += [pltpu.SemaphoreType.DMA((sends,)), pltpu.SemaphoreType.DMA((receives,))]
     sizes = (n_row, n_col, n_layer, ta, bs, nc, chunks, slots, parts, pieces, unroll)

time: 51.3 us -> 51.3 us (level)
  no operation moved by 1% of the time
where the time goes in v4:
time: 51.3 us; the launch traced here: 51.2 us
  Pallas kernels  50.5 us (98%)
  local copies, waits for them, and re-layouts  0.71 us (1%)
    pallas_call x1, Pallas kernels, shards(): pl.pallas_call(functools.partial(kernel, sizes=sizes), out_shape=jax.Shap...  50.5 us

profile of v4, /device:TPU:32, one launch (start us, length us, event | category | flops | bytes accessed | tf_op | source)
XLA Modules:
  0.0 51.2 jit_solution(13388320967524030386)
XLA Ops:
  0.0 50.5 %shard_map.37 = f32[4,128,128]{2,1,0:T(8,128)S(1)} custom-call(s32[3,3,1,256]{3,2,1,0:T(1,128)} %bitcast.7, bf16[16,128,128]{2,1,0:T(8,128)(2,1)} %bitcast.6, bf16[64,128,128]{2,1,0:T(8,128)(2,1)} %bitcast.5), custom_call_target="tpu_custom_call" | custom-call | flops 3221225472 | bytes 3145728 | tf_op jit(solution)/shard_map/pallas_call | solution.py:341
  50.5 0.7 %copy.5 = f32[1,1,4,128,128]{4,3,2,1,0:T(8,128)} copy(f32[1,1,4,128,128]{4,3,2,1,0:T(8,128)S(1)} %bitcast.4) | data formatting | bytes 524288
